TPU v7x, 512 devices: a whole 4x8x8 slice. The times are simulated.
512 devices in a mesh: outer: 128 (over z, y, core), inner: 4 (over x).
Axes of the slice: x: 4, y: 8, z: 8, core: 2. Of those that a mesh axis runs over, the one named last changes fastest.
Arguments:
- query_states: bfloat16 [65536, 4096], P(('outer', 'inner')), may hold values from -6 to 6
- key_states: bfloat16 [65536, 4096], P(('outer', 'inner')), may hold values from -6 to 6
- value_states: bfloat16 [65536, 4096], P(('outer', 'inner')), may hold values from -6 to 6
- doc_lengths: int32 [128], replicated, may hold values from 1 to 1024, 65536 in all
- slopes: float32 [32], replicated, may hold values from 0.00024414062 to 0.0625
Outputs:
- attended: bfloat16 [65536, 4096], P(('outer', 'inner'))
Inputs may be any that keep to these rules, and one draw needn't show every extreme that they name: `doc_lengths`: the lengths add up to 65536; the longest is exactly 1024.
All inputs are finite; a program needn't handle non-finite values.
Results may differ from a plain program's by a relative error of at most 0.0045.
Values may be sent and summed in bfloat16 or wider, within the bound.
No kernel may reach another device: no remote copies, remote signals or barrier semaphores. Data moves between devices by JAX's collectives and lax.ppermute only.
A program may use at most 64 MiB of HBM per device.

v0:
```python
import math
import jax
import jax.numpy as jnp
from jax import lax
from jax.sharding import PartitionSpec as P

SPAN = 2
NEG_FILL = -1e30


def shifted(value, axis, steps):
    count = lax.axis_size(axis)
    first, last = (max(0, -steps), min(count, count - steps))
    return lax.ppermute(value, axis, [(source, source + steps) for source in range(first, last)])


def document_of(positions, doc_lengths):
    boundary = jnp.cumsum(doc_lengths)
    return jnp.sum((boundary[None, :] <= positions[:, None]).astype(jnp.int32), axis=1)


def empty_status(row_count, head_count, head_width):
    return (
        jnp.full((row_count, head_count), NEG_FILL, jnp.float32),
        jnp.zeros((row_count, head_count), jnp.float32),
        jnp.zeros((row_count, head_count, head_width), jnp.float32),
    )


def attend_block(status, query_parts, key_slab, value_slab, key_pos, key_doc, slopes):
    query_rows, query_pos, query_doc = query_parts
    allowed = (query_doc[:, None] == key_doc[None, :]) & (key_pos[None, :] <= query_pos[:, None])

    def update(current):
        running_max, row_total, weighted_sum = current
        scores = jnp.einsum(
            "qhd,khd->qhk", query_rows, key_slab, preferred_element_type=jnp.float32
        )
        scores = scores * (1.0 / math.sqrt(query_rows.shape[-1]))
        distance = (query_pos[:, None] - key_pos[None, :]).astype(jnp.float32)
        scores = scores - slopes[None, :, None] * distance[:, None, :]
        scores = jnp.where(allowed[:, None, :], scores, NEG_FILL)
        new_max = jnp.maximum(running_max, jnp.max(scores, axis=-1))
        weights = jnp.where(allowed[:, None, :], jnp.exp(scores - new_max[:, :, None]), 0.0)
        rescale = jnp.exp(running_max - new_max)
        row_total = row_total * rescale + jnp.sum(weights, axis=-1)
        products = jnp.einsum(
            "qhk,khd->qhd",
            weights.astype(jnp.bfloat16),
            value_slab,
            preferred_element_type=jnp.float32,
        )
        weighted_sum = weighted_sum * rescale[:, :, None] + products
        return (new_max, row_total, weighted_sum)

    def unchanged(current):
        return current

    return lax.cond(jnp.any(allowed), update, unchanged, status)


def attend_keys(status, query_parts, key_slab, value_slab, key_pos, slopes, doc_lengths):
    key_doc = document_of(key_pos, doc_lengths)
    key_count = key_slab.shape[0]
    slab_rows = 256
    pieces = key_count // slab_rows
    stacked = (
        key_slab.reshape((pieces, slab_rows) + key_slab.shape[1:]),
        value_slab.reshape((pieces, slab_rows) + value_slab.shape[1:]),
        key_pos.reshape(pieces, slab_rows),
        key_doc.reshape(pieces, slab_rows),
    )

    def scan_step(current, portion):
        return (
            attend_block(
                current, query_parts, portion[0], portion[1], portion[2], portion[3], slopes
            ),
            None,
        )

    result, unused = lax.scan(scan_step, status, stacked)
    return result


def combine(first_status, second_status):
    new_max = jnp.maximum(first_status[0], second_status[0])
    left_scale = jnp.exp(first_status[0] - new_max)
    right_scale = jnp.exp(second_status[0] - new_max)
    return (
        new_max,
        first_status[1] * left_scale + second_status[1] * right_scale,
        first_status[2] * left_scale[:, :, None] + second_status[2] * right_scale[:, :, None],
    )


def queries_from_later(query_rows, hops_back):
    return shifted(query_rows, "outer", -hops_back)


def partials_home(status, hops_back):
    running_max, row_total, weighted_sum = status
    moved_max, moved_total, moved_sum = shifted(
        (running_max, row_total, weighted_sum), "outer", hops_back
    )
    return (jnp.where(moved_total > 0.0, moved_max, NEG_FILL), moved_total, moved_sum)


def rows_of(status, slot_index, row_count):
    return tuple(
        (member[slot_index * row_count : (slot_index + 1) * row_count] for member in status)
    )


def bring_home(status, row_count, span_count):
    own_status = rows_of(status, 0, row_count)
    distant = [rows_of(status, hops_back, row_count) for hops_back in range(1, span_count + 1)]
    merged = own_status
    for hops_back in range(1, span_count + 1):
        merged = combine(merged, partials_home(distant[hops_back - 1], hops_back))
    return merged


def with_later_queries(own_rows, own_pos, group_rows, span_count, doc_lengths):
    rows_list = [own_rows]
    pos_list = [own_pos]
    for hops_back in range(1, span_count + 1):
        rows_list.append(queries_from_later(own_rows, hops_back))
        pos_list.append(own_pos + hops_back * group_rows)
    all_pos = jnp.concatenate(pos_list)
    return (jnp.concatenate(rows_list, axis=0), all_pos, document_of(all_pos, doc_lengths))


def normalize(status):
    return (status[2] / status[1][:, :, None]).astype(jnp.bfloat16)


def per_device(query_states, key_states, value_states, doc_lengths, slopes):
    rows_dev = query_states.shape[0]
    head_count = slopes.shape[0]
    head_width = query_states.shape[1] // head_count
    inner_count = lax.axis_size("inner")
    group_index = lax.axis_index("outer")
    inner_index = lax.axis_index("inner")
    group_rows = rows_dev * inner_count
    group_start = group_index * group_rows
    own_queries = query_states.reshape(rows_dev, head_count, head_width)
    own_pos = group_start + inner_index * rows_dev + jnp.arange(rows_dev, dtype=jnp.int32)
    query_parts = with_later_queries(own_queries, own_pos, group_rows, SPAN, doc_lengths)
    status = empty_status(query_parts[0].shape[0], head_count, head_width)
    portions = (
        lax.all_gather(
            key_states.reshape(rows_dev, head_count, head_width), "inner", axis=0, tiled=True
        ),
        lax.all_gather(
            value_states.reshape(rows_dev, head_count, head_width), "inner", axis=0, tiled=True
        ),
    )
    key_pos = group_start + jnp.arange(portions[0].shape[0], dtype=jnp.int32)
    status = attend_keys(
        status, query_parts, portions[0], portions[1], key_pos, slopes, doc_lengths
    )
    combined = bring_home(status, rows_dev, SPAN)
    return normalize(combined).reshape(rows_dev, head_count * head_width)


def solution(mesh):
    placed = (
        P(("outer", "inner"), None),
        P(("outer", "inner"), None),
        P(("outer", "inner"), None),
        P(),
        P(),
    )
    return jax.shard_map(
        per_device,
        mesh=mesh,
        in_specs=placed,
        out_specs=P(("outer", "inner"), None),
        check_vma=False,
    )
```

profile of v0, /device:TPU:256, one launch (start us, length us, event | category | flops | bytes accessed | tf_op | source)
XLA Modules:
  0.0 273.0 jit_solution(12478321590578903642)
XLA Ops:
  12.3 3.9 %collective-permute-start = (bf16[128,32,128]{0,2,1:T(8,128)(2,1)S(1)}, bf16[128,32,128]{0,2,1:T(8,128)(2,1)S(1)}, u32[]{:S(2)}, u32[]{:S(2)}) collective-permute-start(bf16[128,32,128]{0,2,1:T(8,128)(2,1)S(1)} %bitcast.49), channel_id=1, source_target_pairs={{4,0},{8,4},{12,8},{16,12},{20,16},{24,20},{28,24},{32,28},{36,32}... | collective-permute-start | bytes 3145736 | tf_op jit(solution)/shard_map/ppermute | solution.py:14
  16.2 3.3 %collective-permute-start.1 = (bf16[128,32,128]{0,2,1:T(8,128)(2,1)S(1)}, bf16[128,32,128]{0,2,1:T(8,128)(2,1)}, u32[]{:S(2)}, u32[]{:S(2)}) collective-permute-start(bf16[128,32,128]{0,2,1:T(8,128)(2,1)S(1)} %bitcast.50), channel_id=1, source_target_pairs={{8,0},{12,4},{16,8},{20,12},{24,16},{28,20},{32,24},{36,28},{40,32... | collective-permute-start | bytes 3145736 | tf_op jit(solution)/shard_map/ppermute | solution.py:14
  20.4 17.2 %collective-permute-done = bf16[128,32,128]{0,2,1:T(8,128)(2,1)S(1)} collective-permute-done((bf16[128,32,128]{0,2,1:T(8,128)(2,1)S(1)}, bf16[128,32,128]{0,2,1:T(8,128)(2,1)S(1)}, u32[]{:S(2)}, u32[]{:S(2)}) %collective-permute-start) | collective-permute-done | bytes 1048608 | tf_op jit(solution)/shard_map/ppermute | solution.py:14
  38.7 12.4 %collective-permute-done.1 = bf16[128,32,128]{0,2,1:T(8,128)(2,1)} collective-permute-done((bf16[128,32,128]{0,2,1:T(8,128)(2,1)S(1)}, bf16[128,32,128]{0,2,1:T(8,128)(2,1)}, u32[]{:S(2)}, u32[]{:S(2)}) %collective-permute-start.1) | collective-permute-done | bytes 1048608 | tf_op jit(solution)/shard_map/ppermute | solution.py:14
  56.4 8.4 %all-gather.3.cloned.1.call-done = bf16[512,32,128]{2,1,0:T(8,128)(2,1)} async-done(((bf16[128,32,128]{2,1,0:T(8,128)(2,1)}), bf16[512,32,128]{2,1,0:T(8,128)(2,1)}) %all-gather.3.cloned.1.call-update) | async-done | bytes 4194320 | tf_op jit(solution)/shard_map/all_gather | solution.py:152
  64.8 5.8 %copy.26 = bf16[2,256,32,128]{3,1,2,0:T(8,128)(2,1)} copy(bf16[2,256,32,128]{3,2,1,0:T(8,128)(2,1)} %bitcast.45) | data formatting | bytes 8388608 | tf_op jit(solution)/shard_map/while | solution.py:82
  70.7 50.3 %all-gather.5.cloned.1.call-done = bf16[512,32,128]{2,1,0:T(8,128)(2,1)} async-done(((bf16[128,32,128]{2,1,0:T(8,128)(2,1)}), bf16[512,32,128]{2,1,0:T(8,128)(2,1)}) %all-gather.5.cloned.1.call-update) | async-done | bytes 4194320 | tf_op jit(solution)/shard_map/all_gather | solution.py:155
  121.0 6.0 %copy.28 = bf16[2,256,32,128]{3,1,2,0:T(8,128)(2,1)} copy(bf16[2,256,32,128]{3,2,1,0:T(8,128)(2,1)} %bitcast.46) | data formatting | bytes 8388608 | tf_op jit(solution)/shard_map/while | solution.py:82
  127.0 3.4 %broadcast_in_dim.61 = f32[384,32,128]{2,0,1:T(8,128)} broadcast(f32[]{:T(128)} %constant.59.clone.1), dimensions={} | broadcast | bytes 6291460 | tf_op jit(solution)/shard_map/broadcast_in_dim | solution.py:26
  130.4 41.3 %while.14 = (s32[]{:T(128)}, f32[384,32]{0,1:T(8,128)S(1)}, f32[384,32]{0,1:T(8,128)S(1)}, f32[384,32,128]{2,0,1:T(8,128)}, s32[384]{0:T(512)S(1)}, /*index=5*/s...) while((s32[]{:T(128)}, f32[384,32]{0,1:T(8,128)S(1)}, ...), condition=%wide.region_9.10_spmd, body=%wide.region_3.9_spmd.sunk | while | flops 1674141696 | bytes 104477920 | solution.py:82
  131.9 19.2 %conditional.2 = ((f32[384,32]{0,1:T(8,128)S(1)}, f32[384,32]{0,1:T(8,128)S(1)}, f32[384,32,128]{2,0,1:T(8,128)})) conditional(s32[]{:T(128)} %convert_element_type.41, (f32[384,32]{0,1:T(8,128)S(1)}, f32[384,32]{0,1:T(8,128)S(1)}, f32[384,32,128]{2,0,1:T(8,128)}) %tuple.50, (pred[384,256]{0,1:T(8,128)(4,1)S(1)}, bf16[2,256,32,128]{3,1,2,0:T(8,128)(2,1)}, ...), branch_computations={%region_5.5_spmd, %region_6.8_spmd} | conditional | flops 1673748480 | bytes 104370152 | solution.py:59
  132.0 4.5 %fusion.3 = (f32[384,32]{0,1:T(8,128)S(1)}, f32[32,256,384]{2,1,0:T(8,128)S(1)}) fusion(f32[384,256]{0,1:T(8,128)S(1)} %subtract_convert_fusion, f32[32]{0:T(128)S(1)} %get-tuple-element.141, pred[384,256]{0,1:T(8,128)(4,1)S(1)} %get-tuple-element.137, bf16[384,32,128]{2,0,1:T(8,128)(2,1)S(1)} %get-tuple-element.140, ...), kind=kOutput, calls=%fused_computation.5 | convolution fusion | flops 821022720 | bytes 18367104 | tf_op jit(solution)/shard_map/while/body/eval_jaxpr/cond/branch_1_fun/qhd,khd->qhk/dot_general | solution.py:36
  136.6 4.3 %fusion.2 = f32[384,32]{0,1:T(8,128)S(1)} fusion(f32[32,256,384]{2,1,0:T(8,128)S(1)} %get-tuple-element.239, f32[384,32]{0,1:T(8,128)S(1)} %max.8, f32[384,256]{0,1:T(8,128)S(1)} %subtract_convert_fusion, f32[32]{0:T(128)S(1)} %get-tuple-element.141, pred[384,256]{0,1:T(8,128)(4,1)S(1)} %get-tuple-element.137), kind=kLoop, calls=%fused_computation.4 | loop fusion | flops 22007808 | bytes 13172864 | tf_op jit(solution)/shard_map/while/body/eval_jaxpr/cond/branch_1_fun/reduce_sum | solution.py:46
  140.9 7.5 %bitcast_add_fusion = f32[384,32,128]{2,0,1:T(8,128)S(1)} fusion(f32[384,32,128]{2,0,1:T(8,128)S(1)} %bitcast.44, f32[384,32]{0,1:T(8,128)S(1)} %get-tuple-element.230, f32[32,256,384]{2,1,0:T(8,128)S(1)} %get-tuple-element.239, f32[384,32]{0,1:T(8,128)S(1)} %max.8, f32[384,256]{0,1:T(8,128)S(1)} %subtract_convert_fusion, f32[32]{0:T(128)S(1)} %get-tuple-element.141, ...), kind=kOutput, calls=%fused_computation.6 | convolution fusion | flops 830472192 | bytes 27853440 | tf_op jit(solution)/shard_map/while/body/eval_jaxpr/cond/branch_1_fun/qhk,khd->qhd/dot_general | solution.py:47
  152.5 19.2 %conditional.2 = ((f32[384,32]{0,1:T(8,128)S(1)}, f32[384,32]{0,1:T(8,128)S(1)}, f32[384,32,128]{2,0,1:T(8,128)})) conditional(s32[]{:T(128)} %convert_element_type.41, (f32[384,32]{0,1:T(8,128)S(1)}, f32[384,32]{0,1:T(8,128)S(1)}, f32[384,32,128]{2,0,1:T(8,128)}) %tuple.50, (pred[384,256]{0,1:T(8,128)(4,1)S(1)}, bf16[2,256,32,128]{3,1,2,0:T(8,128)(2,1)}, ...), branch_computations={%region_5.5_spmd, %region_6.8_spmd} | conditional | flops 1673748480 | bytes 104370152 | solution.py:59
  152.7 4.5 %fusion.3 = (f32[384,32]{0,1:T(8,128)S(1)}, f32[32,256,384]{2,1,0:T(8,128)S(1)}) fusion(f32[384,256]{0,1:T(8,128)S(1)} %subtract_convert_fusion, f32[32]{0:T(128)S(1)} %get-tuple-element.141, pred[384,256]{0,1:T(8,128)(4,1)S(1)} %get-tuple-element.137, bf16[384,32,128]{2,0,1:T(8,128)(2,1)S(1)} %get-tuple-element.140, ...), kind=kOutput, calls=%fused_computation.5 | convolution fusion | flops 821022720 | bytes 18367104 | tf_op jit(solution)/shard_map/while/body/eval_jaxpr/cond/branch_1_fun/qhd,khd->qhk/dot_general | solution.py:36
  157.2 4.3 %fusion.2 = f32[384,32]{0,1:T(8,128)S(1)} fusion(f32[32,256,384]{2,1,0:T(8,128)S(1)} %get-tuple-element.239, f32[384,32]{0,1:T(8,128)S(1)} %max.8, f32[384,256]{0,1:T(8,128)S(1)} %subtract_convert_fusion, f32[32]{0:T(128)S(1)} %get-tuple-element.141, pred[384,256]{0,1:T(8,128)(4,1)S(1)} %get-tuple-element.137), kind=kLoop, calls=%fused_computation.4 | loop fusion | flops 22007808 | bytes 13172864 | tf_op jit(solution)/shard_map/while/body/eval_jaxpr/cond/branch_1_fun/reduce_sum | solution.py:46
  161.6 7.5 %bitcast_add_fusion = f32[384,32,128]{2,0,1:T(8,128)S(1)} fusion(f32[384,32,128]{2,0,1:T(8,128)S(1)} %bitcast.44, f32[384,32]{0,1:T(8,128)S(1)} %get-tuple-element.230, f32[32,256,384]{2,1,0:T(8,128)S(1)} %get-tuple-element.239, f32[384,32]{0,1:T(8,128)S(1)} %max.8, f32[384,256]{0,1:T(8,128)S(1)} %subtract_convert_fusion, f32[32]{0:T(128)S(1)} %get-tuple-element.141, ...), kind=kOutput, calls=%fused_computation.6 | convolution fusion | flops 830472192 | bytes 27853440 | tf_op jit(solution)/shard_map/while/body/eval_jaxpr/cond/branch_1_fun/qhk,khd->qhd/dot_general | solution.py:47
  176.1 3.4 %collective-permute-start.7 = (f32[128,32,128]{2,0,1:T(8,128)S(1)}, f32[128,32,128]{2,0,1:T(8,128)S(1)}, u32[]{:S(2)}, u32[]{:S(2)}) collective-permute-start(f32[128,32,128]{2,0,1:T(8,128)S(1)} %get-tuple-element.243), channel_id=1, source_target_pairs={{0,8},{4,12},{8,16},{12,20},{16,24},{20,28},{24,32},{28,36},{32,40... | collective-permute-start | bytes 6291464 | tf_op jit(solution)/shard_map/ppermute | solution.py:14
  179.6 3.2 %collective-permute-start.2 = (f32[128,32]{0,1:T(8,128)S(1)}, f32[128,32]{0,1:T(8,128)S(1)}, u32[]{:S(2)}, u32[]{:S(2)}) collective-permute-start(f32[128,32]{0,1:T(8,128)S(1)} %get-tuple-element.246), channel_id=1, source_target_pairs={{0,4},{4,8},{8,12},{12,16},{16,20},{20,24},{24,28},{28,32},{32,36}... | collective-permute-start | bytes 49160 | tf_op jit(solution)/shard_map/ppermute | solution.py:14
  185.0 3.4 %collective-permute-start.5 = (f32[128,32]{0,1:T(8,128)S(1)}, f32[128,32]{0,1:T(8,128)S(1)}, u32[]{:S(2)}, u32[]{:S(2)}) collective-permute-start(f32[128,32]{0,1:T(8,128)S(1)} %get-tuple-element.247), channel_id=1, source_target_pairs={{0,8},{4,12},{8,16},{12,20},{16,24},{20,28},{24,32},{28,36},{32,40... | collective-permute-start | bytes 49160 | tf_op jit(solution)/shard_map/ppermute | solution.py:14
  188.4 61.8 %collective-permute-done.2 = f32[128,32]{0,1:T(8,128)S(1)} collective-permute-done((f32[128,32]{0,1:T(8,128)S(1)}, f32[128,32]{0,1:T(8,128)S(1)}, u32[]{:S(2)}, u32[]{:S(2)}) %collective-permute-start.2) | collective-permute-done | bytes 16416 | tf_op jit(solution)/shard_map/ppermute | solution.py:14
  252.1 7.0 %collective-permute-done.6 = f32[128,32]{0,1:T(8,128)S(1)} collective-permute-done((f32[128,32]{0,1:T(8,128)S(1)}, f32[128,32]{0,1:T(8,128)S(1)}, u32[]{:S(2)}, u32[]{:S(2)}) %collective-permute-start.6) | collective-permute-done | bytes 16416 | tf_op jit(solution)/shard_map/ppermute | solution.py:14
  259.2 7.0 %copy_bitcast_fusion = bf16[128,4096]{1,0:T(8,128)(2,1)} fusion(f32[128,32]{0,1:T(8,128)S(1)} %get-tuple-element.233, f32[128,32,128]{2,0,1:T(8,128)S(1)} %collective-permute-done.7, f32[128,32]{0,1:T(8,128)S(1)} %get-tuple-element.237, f32[128,32]{0,1:T(8,128)S(1)} %get-tuple-element.236, f32[128,32,128]{2,0,1:T(8,128)S(1)} %collective-permute-done.4, ...), kind=kLoop, calls=%fused_computation.27 | loop fusion | flops 4194304 | bytes 7421952 | tf_op jit(solution)/shard_map/reshape | solution.py:164
  (71 shorter events, 28.8 us)
Async XLA Ops:
  6.5 5.1 %copy-start.3 = (bf16[128,4096]{1,0:T(8,128)(2,1)S(1)}, bf16[128,4096]{1,0:T(8,128)(2,1)}, u32[]{:S(2)}) copy-start(bf16[128,4096]{1,0:T(8,128)(2,1)} %param.9) | copy-start | bytes 3145732
  6.5 12.9 %copy-start.6 = (s32[128]{0:T(128)S(1)}, s32[128]{0:T(128)}, u32[]{:S(2)}) copy-start(s32[128]{0:T(128)} %param.12) | copy-start | bytes 1540
  6.5 58.3 %all-gather.3.cloned.1.call-start = ((), (), s32[]{:S(2)}) async-start(), calls=%async_computation | async-start | bytes 5242880 | tf_op jit(solution)/shard_map/all_gather | solution.py:152
  9.1 111.9 %all-gather.5.cloned.1.call-start = ((), (), s32[]{:S(2)}) async-start(), calls=%async_computation.1 | async-start | bytes 5242880 | tf_op jit(solution)/shard_map/all_gather | solution.py:155
  12.3 25.4 %copy-start.1 = (bf16[128,4096]{0,1:T(8,128)(2,1)}, bf16[128,4096]{0,1:T(8,128)(2,1)S(1)}, u32[]{:S(2)}) copy-start(bf16[128,4096]{0,1:T(8,128)(2,1)S(1)} %copy.25) | copy-start | bytes 3145732
  12.3 25.4 %collective-permute-start = (bf16[128,32,128]{0,2,1:T(8,128)(2,1)S(1)}, bf16[128,32,128]{0,2,1:T(8,128)(2,1)S(1)}, u32[]{:S(2)}, u32[]{:S(2)}) collective-permute-start(bf16[128,32,128]{0,2,1:T(8,128)(2,1)S(1)} %bitcast.49), channel_id=1, source_target_pairs={{4,0},{8,4},{12,8},{16,12},{20,16},{24,20},{28,24},{32,28},{36,32}... | collective-permute-start | bytes 3145736 | tf_op jit(solution)/shard_map/ppermute | solution.py:14
  16.2 34.9 %collective-permute-start.1 = (bf16[128,32,128]{0,2,1:T(8,128)(2,1)S(1)}, bf16[128,32,128]{0,2,1:T(8,128)(2,1)}, u32[]{:S(2)}, u32[]{:S(2)}) collective-permute-start(bf16[128,32,128]{0,2,1:T(8,128)(2,1)S(1)} %bitcast.50), channel_id=1, source_target_pairs={{8,0},{12,4},{16,8},{20,12},{24,16},{28,20},{32,24},{36,28},{40,32... | collective-permute-start | bytes 3145736 | tf_op jit(solution)/shard_map/ppermute | solution.py:14
  37.6 1.0 copy-start.4
  121.0 9.4 %copy-start.2 = (bf16[384,32,128]{2,0,1:T(8,128)(2,1)S(1)}, bf16[384,32,128]{2,0,1:T(8,128)(2,1)}, u32[]{:S(2)}) copy-start(bf16[384,32,128]{2,0,1:T(8,128)(2,1)} %copy.27) | copy-start | bytes 9437188
  121.0 9.4 %copy-start.5 = (f32[32]{0:T(128)S(1)}, f32[32]{0:T(128)}, u32[]{:S(2)}) copy-start(f32[32]{0:T(128)} %param.13) | copy-start | bytes 388
  131.9 9.0 %slice-start = ((s8[6291456]{0:T(1024)(128)(4,1)}), s8[4194304]{0:T(1024)(128)(4,1)S(1)}, s32[]{:S(2)}) async-start(s8[6291456]{0:T(1024)(128)(4,1)} %bitcast.43), calls=%async_computation.2 | async-start | bytes 8388608 | tf_op jit(solution)/shard_map/while/body/eval_jaxpr/cond
  132.0 8.9 %slice-start.1 = ((s8[6291456]{0:T(1024)(128)(4,1)}), s8[2097152]{0:T(1024)(128)(4,1)S(1)}, s32[]{:S(2)}) async-start(s8[6291456]{0:T(1024)(128)(4,1)} %bitcast.43), calls=%async_computation.3 | async-start | bytes 4194304 | tf_op jit(solution)/shard_map/while/body/eval_jaxpr/cond
  148.4 2.7 copy-start
  152.5 9.0 %slice-start = ((s8[6291456]{0:T(1024)(128)(4,1)}), s8[4194304]{0:T(1024)(128)(4,1)S(1)}, s32[]{:S(2)}) async-start(s8[6291456]{0:T(1024)(128)(4,1)} %bitcast.43), calls=%async_computation.2 | async-start | bytes 8388608 | tf_op jit(solution)/shard_map/while/body/eval_jaxpr/cond
  152.7 8.9 %slice-start.1 = ((s8[6291456]{0:T(1024)(128)(4,1)}), s8[2097152]{0:T(1024)(128)(4,1)S(1)}, s32[]{:S(2)}) async-start(s8[6291456]{0:T(1024)(128)(4,1)} %bitcast.43), calls=%async_computation.3 | async-start | bytes 4194304 | tf_op jit(solution)/shard_map/while/body/eval_jaxpr/cond
  169.0 2.7 copy-start
  174.2 84.9 %collective-permute-start.4 = (f32[128,32,128]{2,0,1:T(8,128)S(1)}, f32[128,32,128]{2,0,1:T(8,128)S(1)}, u32[]{:S(2)}, u32[]{:S(2)}) collective-permute-start(f32[128,32,128]{2,0,1:T(8,128)S(1)} %get-tuple-element.242), channel_id=1, source_target_pairs={{0,4},{4,8},{8,12},{12,16},{16,20},{20,24},{24,28},{28,32},{32,36}... | collective-permute-start | bytes 6291464 | tf_op jit(solution)/shard_map/ppermute | solution.py:14
  176.1 83.0 %collective-permute-start.7 = (f32[128,32,128]{2,0,1:T(8,128)S(1)}, f32[128,32,128]{2,0,1:T(8,128)S(1)}, u32[]{:S(2)}, u32[]{:S(2)}) collective-permute-start(f32[128,32,128]{2,0,1:T(8,128)S(1)} %get-tuple-element.243), channel_id=1, source_target_pairs={{0,8},{4,12},{8,16},{12,20},{16,24},{20,28},{24,32},{28,36},{32,40... | collective-permute-start | bytes 6291464 | tf_op jit(solution)/shard_map/ppermute | solution.py:14
  179.6 70.6 %collective-permute-start.2 = (f32[128,32]{0,1:T(8,128)S(1)}, f32[128,32]{0,1:T(8,128)S(1)}, u32[]{:S(2)}, u32[]{:S(2)}) collective-permute-start(f32[128,32]{0,1:T(8,128)S(1)} %get-tuple-element.246), channel_id=1, source_target_pairs={{0,4},{4,8},{8,12},{12,16},{16,20},{20,24},{24,28},{28,32},{32,36}... | collective-permute-start | bytes 49160 | tf_op jit(solution)/shard_map/ppermute | solution.py:14
  182.8 69.3 %collective-permute-start.3 = (f32[128,32]{0,1:T(8,128)S(1)}, f32[128,32]{0,1:T(8,128)S(1)}, u32[]{:S(2)}, u32[]{:S(2)}) collective-permute-start(f32[128,32]{0,1:T(8,128)S(1)} %get-tuple-element.245), channel_id=1, source_target_pairs={{0,4},{4,8},{8,12},{12,16},{16,20},{20,24},{24,28},{28,32},{32,36}... | collective-permute-start | bytes 49160 | tf_op jit(solution)/shard_map/ppermute | solution.py:14
  185.0 67.1 %collective-permute-start.5 = (f32[128,32]{0,1:T(8,128)S(1)}, f32[128,32]{0,1:T(8,128)S(1)}, u32[]{:S(2)}, u32[]{:S(2)}) collective-permute-start(f32[128,32]{0,1:T(8,128)S(1)} %get-tuple-element.247), channel_id=1, source_target_pairs={{0,8},{4,12},{8,16},{12,20},{16,24},{20,28},{24,32},{28,36},{32,40... | collective-permute-start | bytes 49160 | tf_op jit(solution)/shard_map/ppermute | solution.py:14
  250.2 8.9 %collective-permute-start.6 = (f32[128,32]{0,1:T(8,128)S(1)}, f32[128,32]{0,1:T(8,128)S(1)}, u32[]{:S(2)}, u32[]{:S(2)}) collective-permute-start(f32[128,32]{0,1:T(8,128)S(1)} %get-tuple-element.244), channel_id=1, source_target_pairs={{0,8},{4,12},{8,16},{12,20},{16,24},{20,28},{24,32},{28,36},{32,40... | collective-permute-start | bytes 49160 | tf_op jit(solution)/shard_map/ppermute | solution.py:14
Sparse Core Ops, SparseCore 0:
  9.5 55.3 all-gather.2
  66.9 53.9 all-gather.4
where the time goes:
time: 274 us; the launch traced here: 273 us
  waiting for transfers between devices  157 us (57%)
  local copies, waits for them, and re-layouts  32.9 us (12%)
  matrix products  24 us (9%)
  starting transfers between devices  23.2 us (8%)
  other arithmetic  20.6 us (8%)
  between operations  13.6 us (5%)
    ppermute x8, waiting for transfers between devices, shifted(): lax.ppermute(value, axis, [(source, source + steps) for source in range(f...  98.4 us
    all_gather x1, waiting for transfers between devices, per_device(): lax.all_gather(value_states.reshape(rows_dev, head_count, head_width), 'i...  50.3 us
    ppermute x8, starting transfers between devices, shifted(): lax.ppermute(value, axis, [(source, source + steps) for source in range(f...  23.2 us
    dot_general x2, matrix products, update(): jnp.einsum('qhk,khd->qhd', weights.astype(jnp.bfloat16), value_slab, pref...  15 us
    while x3, local copies, waits for them, and re-layouts, attend_keys(): result, unused = lax.scan(scan_step, status, stacked)  14.8 us
    dot_general x2, matrix products, update(): jnp.einsum('qhd,khd->qhk', query_rows, key_slab, preferred_element_type=j...  9.01 us
    reduce_sum x2, other arithmetic, update(): row_total = row_total * rescale + jnp.sum(weights, axis=-1)  8.57 us
    all_gather x1, waiting for transfers between devices, per_device(): lax.all_gather(key_states.reshape(rows_dev, head_count, head_width), 'inn...  8.4 us
  transfers between devices with their start and end apart: 10, of which 6 were waited for; matrix products, arithmetic and copies ran while one was open for 6% of the time, Pallas kernels for 0%

commit v1 on v0

--- a/solution.py
+++ b/solution.py
@@ -152,8 +152,17 @@
         lax.all_gather(
             key_states.reshape(rows_dev, head_count, head_width), "inner", axis=0, tiled=True
         ),
-        lax.all_gather(
-            value_states.reshape(rows_dev, head_count, head_width), "inner", axis=0, tiled=True
+        jnp.concatenate(
+            lax.all_to_all(
+                jnp.stack(
+                    [value_states.reshape(rows_dev, head_count, head_width)]
+                    * lax.axis_size("inner")
+                ),
+                "inner",
+                0,
+                0,
+            ),
+            axis=0,
         ),
     )
     key_pos = group_start + jnp.arange(portions[0].shape[0], dtype=jnp.int32)

time: 274 us -> 260 us (0.949)
  waiting for transfers between devices: 157 us -> 136 us
  starting transfers between devices: 23.2 us -> 28.5 us
    all_gather x1 -> x0, waiting for transfers between devices: 50.3 us -> none  [per_device(): lax.all_gather(value_states.reshape(rows_dev, head_count, head_width), 'i...]
    all_to_all x0 -> x1, waiting for transfers between devices: none -> 37.9 us  [per_device(): lax.all_to_all(jnp.stack([value_states.reshape(rows_dev, head_count, head...]
    all_gather x1, waiting for transfers between devices: 8.4 us -> 0.01 us  [per_device(): lax.all_gather(key_states.reshape(rows_dev, head_count, head_width), 'inn...]
    all_to_all x0 -> x1, starting transfers between devices: none -> 4.97 us  [per_device(): lax.all_to_all(jnp.stack([value_states.reshape(rows_dev, head_count, head...]
  transfers between devices with their start and end apart: 10 -> 10, of which waited for: 6 -> 5; matrix products, arithmetic and copies ran while one was open for 6% -> 7% of each run, Pallas kernels for 0% -> 0%
where the time goes in v1:
time: 260 us; the launch traced here: 259 us
  waiting for transfers between devices  136 us (52%)
  local copies, waits for them, and re-layouts  34.5 us (13%)
  starting transfers between devices  28.5 us (11%)
  matrix products  24 us (9%)
  other arithmetic  20.5 us (8%)
  between operations  13.6 us (5%)
    ppermute x8, waiting for transfers between devices, shifted(): lax.ppermute(value, axis, [(source, source + steps) for source in range(f...  98.2 us
    all_to_all x1, waiting for transfers between devices, per_device(): lax.all_to_all(jnp.stack([value_states.reshape(rows_dev, head_count, head...  37.9 us
    ppermute x8, starting transfers between devices, shifted(): lax.ppermute(value, axis, [(source, source + steps) for source in range(f...  23.5 us
    dot_general x2, matrix products, update(): jnp.einsum('qhk,khd->qhd', weights.astype(jnp.bfloat16), value_slab, pref...  15 us
    while x3, local copies, waits for them, and re-layouts, attend_keys(): result, unused = lax.scan(scan_step, status, stacked)  14.9 us
    dot_general x2, matrix products, update(): jnp.einsum('qhd,khd->qhk', query_rows, key_slab, preferred_element_type=j...  9.02 us
    reduce_sum x2, other arithmetic, update(): row_total = row_total * rescale + jnp.sum(weights, axis=-1)  8.57 us
    reshape x1, other arithmetic, per_device(): return normalize(combined).reshape(rows_dev, head_count * head_width)  6.98 us
  transfers between devices with their start and end apart: 10, of which 5 were waited for; matrix products, arithmetic and copies ran while one was open for 7% of the time, Pallas kernels for 0%

profile of v1, /device:TPU:256, one launch (start us, length us, event | category | flops | bytes accessed | tf_op | source)
XLA Modules:
  0.0 258.8 jit_solution(17096342022326641731)
XLA Ops:
  13.1 5.0 %all-to-all-start = ((bf16[4,128,32,128]{3,2,1,0:T(8,128)(2,1)}), bf16[4,128,32,128]{3,2,1,0:T(8,128)(2,1)}, u32[]{:S(2)}, u32[]{:S(2)}) async-start(bf16[4,128,32,128]{3,2,1,0:T(8,128)(2,1)} %stack.3), calls=%async_computation | async-start | bytes 8388608 | tf_op jit(solution)/shard_map/all_to_all | solution.py:156
  18.8 3.9 %collective-permute-start = (bf16[128,32,128]{0,2,1:T(8,128)(2,1)S(1)}, bf16[128,32,128]{0,2,1:T(8,128)(2,1)S(1)}, u32[]{:S(2)}, u32[]{:S(2)}) collective-permute-start(bf16[128,32,128]{0,2,1:T(8,128)(2,1)S(1)} %bitcast.48), channel_id=1, source_target_pairs={{4,0},{8,4},{12,8},{16,12},{20,16},{24,20},{28,24},{32,28},{36,32}... | collective-permute-start | bytes 3145736 | tf_op jit(solution)/shard_map/ppermute | solution.py:14
  22.7 3.3 %collective-permute-start.1 = (bf16[128,32,128]{0,2,1:T(8,128)(2,1)S(1)}, bf16[128,32,128]{0,2,1:T(8,128)(2,1)}, u32[]{:S(2)}, u32[]{:S(2)}) collective-permute-start(bf16[128,32,128]{0,2,1:T(8,128)(2,1)S(1)} %bitcast.49), channel_id=1, source_target_pairs={{8,0},{12,4},{16,8},{20,12},{24,16},{28,20},{32,24},{36,28},{40,32... | collective-permute-start | bytes 3145736 | tf_op jit(solution)/shard_map/ppermute | solution.py:14
  26.9 17.2 %collective-permute-done = bf16[128,32,128]{0,2,1:T(8,128)(2,1)S(1)} collective-permute-done((bf16[128,32,128]{0,2,1:T(8,128)(2,1)S(1)}, bf16[128,32,128]{0,2,1:T(8,128)(2,1)S(1)}, u32[]{:S(2)}, u32[]{:S(2)}) %collective-permute-start) | collective-permute-done | bytes 1048608 | tf_op jit(solution)/shard_map/ppermute | solution.py:14
  45.1 12.5 %collective-permute-done.1 = bf16[128,32,128]{0,2,1:T(8,128)(2,1)} collective-permute-done((bf16[128,32,128]{0,2,1:T(8,128)(2,1)S(1)}, bf16[128,32,128]{0,2,1:T(8,128)(2,1)}, u32[]{:S(2)}, u32[]{:S(2)}) %collective-permute-start.1) | collective-permute-done | bytes 1048608 | tf_op jit(solution)/shard_map/ppermute | solution.py:14
  63.0 37.9 %all-to-all-done = bf16[4,128,32,128]{3,2,1,0:T(8,128)(2,1)} async-done(((bf16[4,128,32,128]{3,2,1,0:T(8,128)(2,1)}), bf16[4,128,32,128]{3,2,1,0:T(8,128)(2,1)}, u32[]{:S(2)}, u32[]{:S(2)}) %all-to-all-start) | async-done | bytes 4194336 | tf_op jit(solution)/shard_map/all_to_all | solution.py:156
  100.9 5.8 %copy.28 = bf16[2,256,32,128]{3,1,2,0:T(8,128)(2,1)} copy(bf16[2,256,32,128]{3,2,1,0:T(8,128)(2,1)} %bitcast.9) | data formatting | bytes 8388608 | tf_op jit(solution)/shard_map/while | solution.py:82
  106.8 6.0 %copy.26 = bf16[2,256,32,128]{3,1,2,0:T(8,128)(2,1)} copy(bf16[2,256,32,128]{3,2,1,0:T(8,128)(2,1)} %bitcast.46) | data formatting | bytes 8388608 | tf_op jit(solution)/shard_map/while | solution.py:82
  112.8 3.4 %broadcast_in_dim.61 = f32[384,32,128]{2,0,1:T(8,128)} broadcast(f32[]{:T(128)} %constant.59.clone.1), dimensions={} | broadcast | bytes 6291460 | tf_op jit(solution)/shard_map/broadcast_in_dim | solution.py:26
  116.2 41.3 %while.14 = (s32[]{:T(128)}, f32[384,32]{0,1:T(8,128)S(1)}, f32[384,32]{0,1:T(8,128)S(1)}, f32[384,32,128]{2,0,1:T(8,128)}, s32[384]{0:T(512)S(1)}, /*index=5*/s...) while((s32[]{:T(128)}, f32[384,32]{0,1:T(8,128)S(1)}, ...), condition=%wide.region_9.10_spmd, body=%wide.region_3.9_spmd.sunk | while | flops 1674141696 | bytes 104477920 | solution.py:82
  117.7 19.2 %conditional.2 = ((f32[384,32]{0,1:T(8,128)S(1)}, f32[384,32]{0,1:T(8,128)S(1)}, f32[384,32,128]{2,0,1:T(8,128)})) conditional(s32[]{:T(128)} %convert_element_type.41, (f32[384,32]{0,1:T(8,128)S(1)}, f32[384,32]{0,1:T(8,128)S(1)}, f32[384,32,128]{2,0,1:T(8,128)}) %tuple.50, (pred[384,256]{0,1:T(8,128)(4,1)S(1)}, bf16[2,256,32,128]{3,1,2,0:T(8,128)(2,1)}, ...), branch_computations={%region_5.5_spmd, %region_6.8_spmd} | conditional | flops 1673748480 | bytes 104370152 | solution.py:59
  117.8 4.5 %fusion.3 = (f32[384,32]{0,1:T(8,128)S(1)}, f32[32,256,384]{2,1,0:T(8,128)S(1)}) fusion(f32[384,256]{0,1:T(8,128)S(1)} %subtract_convert_fusion, f32[32]{0:T(128)S(1)} %get-tuple-element.141, pred[384,256]{0,1:T(8,128)(4,1)S(1)} %get-tuple-element.137, bf16[384,32,128]{2,0,1:T(8,128)(2,1)S(1)} %get-tuple-element.140, ...), kind=kOutput, calls=%fused_computation.5 | convolution fusion | flops 821022720 | bytes 18367104 | tf_op jit(solution)/shard_map/while/body/eval_jaxpr/cond/branch_1_fun/qhd,khd->qhk/dot_general | solution.py:36
  122.4 4.3 %fusion.2 = f32[384,32]{0,1:T(8,128)S(1)} fusion(f32[32,256,384]{2,1,0:T(8,128)S(1)} %get-tuple-element.239, f32[384,32]{0,1:T(8,128)S(1)} %max.8, f32[384,256]{0,1:T(8,128)S(1)} %subtract_convert_fusion, f32[32]{0:T(128)S(1)} %get-tuple-element.141, pred[384,256]{0,1:T(8,128)(4,1)S(1)} %get-tuple-element.137), kind=kLoop, calls=%fused_computation.4 | loop fusion | flops 22007808 | bytes 13172864 | tf_op jit(solution)/shard_map/while/body/eval_jaxpr/cond/branch_1_fun/reduce_sum | solution.py:46
  126.7 7.5 %bitcast_add_fusion = f32[384,32,128]{2,0,1:T(8,128)S(1)} fusion(f32[384,32,128]{2,0,1:T(8,128)S(1)} %bitcast.44, f32[384,32]{0,1:T(8,128)S(1)} %get-tuple-element.230, f32[32,256,384]{2,1,0:T(8,128)S(1)} %get-tuple-element.239, f32[384,32]{0,1:T(8,128)S(1)} %max.8, f32[384,256]{0,1:T(8,128)S(1)} %subtract_convert_fusion, f32[32]{0:T(128)S(1)} %get-tuple-element.141, ...), kind=kOutput, calls=%fused_computation.6 | convolution fusion | flops 830472192 | bytes 27853440 | tf_op jit(solution)/shard_map/while/body/eval_jaxpr/cond/branch_1_fun/qhk,khd->qhd/dot_general | solution.py:47
  138.3 19.2 %conditional.2 = ((f32[384,32]{0,1:T(8,128)S(1)}, f32[384,32]{0,1:T(8,128)S(1)}, f32[384,32,128]{2,0,1:T(8,128)})) conditional(s32[]{:T(128)} %convert_element_type.41, (f32[384,32]{0,1:T(8,128)S(1)}, f32[384,32]{0,1:T(8,128)S(1)}, f32[384,32,128]{2,0,1:T(8,128)}) %tuple.50, (pred[384,256]{0,1:T(8,128)(4,1)S(1)}, bf16[2,256,32,128]{3,1,2,0:T(8,128)(2,1)}, ...), branch_computations={%region_5.5_spmd, %region_6.8_spmd} | conditional | flops 1673748480 | bytes 104370152 | solution.py:59
  138.5 4.5 %fusion.3 = (f32[384,32]{0,1:T(8,128)S(1)}, f32[32,256,384]{2,1,0:T(8,128)S(1)}) fusion(f32[384,256]{0,1:T(8,128)S(1)} %subtract_convert_fusion, f32[32]{0:T(128)S(1)} %get-tuple-element.141, pred[384,256]{0,1:T(8,128)(4,1)S(1)} %get-tuple-element.137, bf16[384,32,128]{2,0,1:T(8,128)(2,1)S(1)} %get-tuple-element.140, ...), kind=kOutput, calls=%fused_computation.5 | convolution fusion | flops 821022720 | bytes 18367104 | tf_op jit(solution)/shard_map/while/body/eval_jaxpr/cond/branch_1_fun/qhd,khd->qhk/dot_general | solution.py:36
  143.0 4.3 %fusion.2 = f32[384,32]{0,1:T(8,128)S(1)} fusion(f32[32,256,384]{2,1,0:T(8,128)S(1)} %get-tuple-element.239, f32[384,32]{0,1:T(8,128)S(1)} %max.8, f32[384,256]{0,1:T(8,128)S(1)} %subtract_convert_fusion, f32[32]{0:T(128)S(1)} %get-tuple-element.141, pred[384,256]{0,1:T(8,128)(4,1)S(1)} %get-tuple-element.137), kind=kLoop, calls=%fused_computation.4 | loop fusion | flops 22007808 | bytes 13172864 | tf_op jit(solution)/shard_map/while/body/eval_jaxpr/cond/branch_1_fun/reduce_sum | solution.py:46
  147.4 7.5 %bitcast_add_fusion = f32[384,32,128]{2,0,1:T(8,128)S(1)} fusion(f32[384,32,128]{2,0,1:T(8,128)S(1)} %bitcast.44, f32[384,32]{0,1:T(8,128)S(1)} %get-tuple-element.230, f32[32,256,384]{2,1,0:T(8,128)S(1)} %get-tuple-element.239, f32[384,32]{0,1:T(8,128)S(1)} %max.8, f32[384,256]{0,1:T(8,128)S(1)} %subtract_convert_fusion, f32[32]{0:T(128)S(1)} %get-tuple-element.141, ...), kind=kOutput, calls=%fused_computation.6 | convolution fusion | flops 830472192 | bytes 27853440 | tf_op jit(solution)/shard_map/while/body/eval_jaxpr/cond/branch_1_fun/qhk,khd->qhd/dot_general | solution.py:47
  162.0 3.5 %collective-permute-start.7 = (f32[128,32,128]{2,0,1:T(8,128)S(1)}, f32[128,32,128]{2,0,1:T(8,128)S(1)}, u32[]{:S(2)}, u32[]{:S(2)}) collective-permute-start(f32[128,32,128]{2,0,1:T(8,128)S(1)} %get-tuple-element.243), channel_id=1, source_target_pairs={{0,8},{4,12},{8,16},{12,20},{16,24},{20,28},{24,32},{28,36},{32,40... | collective-permute-start | bytes 6291464 | tf_op jit(solution)/shard_map/ppermute | solution.py:14
  165.5 3.3 %collective-permute-start.2 = (f32[128,32]{0,1:T(8,128)S(1)}, f32[128,32]{0,1:T(8,128)S(1)}, u32[]{:S(2)}, u32[]{:S(2)}) collective-permute-start(f32[128,32]{0,1:T(8,128)S(1)} %get-tuple-element.246), channel_id=1, source_target_pairs={{0,4},{4,8},{8,12},{12,16},{16,20},{20,24},{24,28},{28,32},{32,36}... | collective-permute-start | bytes 49160 | tf_op jit(solution)/shard_map/ppermute | solution.py:14
  171.0 3.5 %collective-permute-start.5 = (f32[128,32]{0,1:T(8,128)S(1)}, f32[128,32]{0,1:T(8,128)S(1)}, u32[]{:S(2)}, u32[]{:S(2)}) collective-permute-start(f32[128,32]{0,1:T(8,128)S(1)} %get-tuple-element.247), channel_id=1, source_target_pairs={{0,8},{4,12},{8,16},{12,20},{16,24},{20,28},{24,32},{28,36},{32,40... | collective-permute-start | bytes 49160 | tf_op jit(solution)/shard_map/ppermute | solution.py:14
  174.5 61.5 %collective-permute-done.2 = f32[128,32]{0,1:T(8,128)S(1)} collective-permute-done((f32[128,32]{0,1:T(8,128)S(1)}, f32[128,32]{0,1:T(8,128)S(1)}, u32[]{:S(2)}, u32[]{:S(2)}) %collective-permute-start.2) | collective-permute-done | bytes 16416 | tf_op jit(solution)/shard_map/ppermute | solution.py:14
  238.0 7.0 %collective-permute-done.6 = f32[128,32]{0,1:T(8,128)S(1)} collective-permute-done((f32[128,32]{0,1:T(8,128)S(1)}, f32[128,32]{0,1:T(8,128)S(1)}, u32[]{:S(2)}, u32[]{:S(2)}) %collective-permute-start.6) | collective-permute-done | bytes 16416 | tf_op jit(solution)/shard_map/ppermute | solution.py:14
  245.0 7.0 %copy_bitcast_fusion = bf16[128,4096]{1,0:T(8,128)(2,1)} fusion(f32[128,32]{0,1:T(8,128)S(1)} %get-tuple-element.233, f32[128,32,128]{2,0,1:T(8,128)S(1)} %collective-permute-done.7, f32[128,32]{0,1:T(8,128)S(1)} %get-tuple-element.237, f32[128,32]{0,1:T(8,128)S(1)} %get-tuple-element.236, f32[128,32,128]{2,0,1:T(8,128)S(1)} %collective-permute-done.4, ...), kind=kLoop, calls=%fused_computation.27 | loop fusion | flops 4194304 | bytes 7421952 | tf_op jit(solution)/shard_map/reshape | solution.py:173
  (71 shorter events, 30.3 us)
Async XLA Ops:
  6.5 100.2 %all-gather.2.cloned.1.call-start = ((), (), s32[]{:S(2)}) async-start(), calls=%async_computation.1 | async-start | bytes 5242880 | tf_op jit(solution)/shard_map/all_gather | solution.py:152
  10.4 7.6 %copy-start.3 = (bf16[128,4096]{1,0:T(8,128)(2,1)S(1)}, bf16[128,4096]{1,0:T(8,128)(2,1)}, u32[]{:S(2)}) copy-start(bf16[128,4096]{1,0:T(8,128)(2,1)} %param.9) | copy-start | bytes 3145732
  13.1 12.9 %copy-start.6 = (s32[128]{0:T(128)S(1)}, s32[128]{0:T(128)}, u32[]{:S(2)}) copy-start(s32[128]{0:T(128)} %param.12) | copy-start | bytes 1540
  13.1 87.8 %all-to-all-start = ((bf16[4,128,32,128]{3,2,1,0:T(8,128)(2,1)}), bf16[4,128,32,128]{3,2,1,0:T(8,128)(2,1)}, u32[]{:S(2)}, u32[]{:S(2)}) async-start(bf16[4,128,32,128]{3,2,1,0:T(8,128)(2,1)} %stack.3), calls=%async_computation | async-start | bytes 8388608 | tf_op jit(solution)/shard_map/all_to_all | solution.py:156
  18.8 25.4 %copy-start.1 = (bf16[128,4096]{0,1:T(8,128)(2,1)}, bf16[128,4096]{0,1:T(8,128)(2,1)S(1)}, u32[]{:S(2)}) copy-start(bf16[128,4096]{0,1:T(8,128)(2,1)S(1)} %copy.25) | copy-start | bytes 3145732
  18.8 25.4 %collective-permute-start = (bf16[128,32,128]{0,2,1:T(8,128)(2,1)S(1)}, bf16[128,32,128]{0,2,1:T(8,128)(2,1)S(1)}, u32[]{:S(2)}, u32[]{:S(2)}) collective-permute-start(bf16[128,32,128]{0,2,1:T(8,128)(2,1)S(1)} %bitcast.48), channel_id=1, source_target_pairs={{4,0},{8,4},{12,8},{16,12},{20,16},{24,20},{28,24},{32,28},{36,32}... | collective-permute-start | bytes 3145736 | tf_op jit(solution)/shard_map/ppermute | solution.py:14
  22.7 34.9 %collective-permute-start.1 = (bf16[128,32,128]{0,2,1:T(8,128)(2,1)S(1)}, bf16[128,32,128]{0,2,1:T(8,128)(2,1)}, u32[]{:S(2)}, u32[]{:S(2)}) collective-permute-start(bf16[128,32,128]{0,2,1:T(8,128)(2,1)S(1)} %bitcast.49), channel_id=1, source_target_pairs={{8,0},{12,4},{16,8},{20,12},{24,16},{28,20},{32,24},{36,28},{40,32... | collective-permute-start | bytes 3145736 | tf_op jit(solution)/shard_map/ppermute | solution.py:14
  44.1 1.0 copy-start.4
  106.8 9.4 %copy-start.2 = (bf16[384,32,128]{2,0,1:T(8,128)(2,1)S(1)}, bf16[384,32,128]{2,0,1:T(8,128)(2,1)}, u32[]{:S(2)}) copy-start(bf16[384,32,128]{2,0,1:T(8,128)(2,1)} %copy.27) | copy-start | bytes 9437188
  106.8 9.4 %copy-start.5 = (f32[32]{0:T(128)S(1)}, f32[32]{0:T(128)}, u32[]{:S(2)}) copy-start(f32[32]{0:T(128)} %param.13) | copy-start | bytes 388
  117.7 9.0 %slice-start = ((s8[6291456]{0:T(1024)(128)(4,1)}), s8[4194304]{0:T(1024)(128)(4,1)S(1)}, s32[]{:S(2)}) async-start(s8[6291456]{0:T(1024)(128)(4,1)} %bitcast.43), calls=%async_computation.2 | async-start | bytes 8388608 | tf_op jit(solution)/shard_map/while/body/eval_jaxpr/cond
  117.8 8.9 %slice-start.1 = ((s8[6291456]{0:T(1024)(128)(4,1)}), s8[2097152]{0:T(1024)(128)(4,1)S(1)}, s32[]{:S(2)}) async-start(s8[6291456]{0:T(1024)(128)(4,1)} %bitcast.43), calls=%async_computation.3 | async-start | bytes 4194304 | tf_op jit(solution)/shard_map/while/body/eval_jaxpr/cond
  134.2 2.7 %copy-start = (f32[384,32,128]{2,0,1:T(8,128)}, f32[384,32,128]{2,0,1:T(8,128)S(1)}, u32[]{:S(2)}) copy-start(f32[384,32,128]{2,0,1:T(8,128)S(1)} %bitcast_add_fusion) | copy-start | bytes 18874372 | tf_op jit(solution)/shard_map/while/body/eval_jaxpr/cond
  138.4 9.0 %slice-start = ((s8[6291456]{0:T(1024)(128)(4,1)}), s8[4194304]{0:T(1024)(128)(4,1)S(1)}, s32[]{:S(2)}) async-start(s8[6291456]{0:T(1024)(128)(4,1)} %bitcast.43), calls=%async_computation.2 | async-start | bytes 8388608 | tf_op jit(solution)/shard_map/while/body/eval_jaxpr/cond
  138.5 8.9 %slice-start.1 = ((s8[6291456]{0:T(1024)(128)(4,1)}), s8[2097152]{0:T(1024)(128)(4,1)S(1)}, s32[]{:S(2)}) async-start(s8[6291456]{0:T(1024)(128)(4,1)} %bitcast.43), calls=%async_computation.3 | async-start | bytes 4194304 | tf_op jit(solution)/shard_map/while/body/eval_jaxpr/cond
  154.9 2.7 %copy-start = (f32[384,32,128]{2,0,1:T(8,128)}, f32[384,32,128]{2,0,1:T(8,128)S(1)}, u32[]{:S(2)}) copy-start(f32[384,32,128]{2,0,1:T(8,128)S(1)} %bitcast_add_fusion) | copy-start | bytes 18874372 | tf_op jit(solution)/shard_map/while/body/eval_jaxpr/cond
  160.0 84.9 %collective-permute-start.4 = (f32[128,32,128]{2,0,1:T(8,128)S(1)}, f32[128,32,128]{2,0,1:T(8,128)S(1)}, u32[]{:S(2)}, u32[]{:S(2)}) collective-permute-start(f32[128,32,128]{2,0,1:T(8,128)S(1)} %get-tuple-element.242), channel_id=1, source_target_pairs={{0,4},{4,8},{8,12},{12,16},{16,20},{20,24},{24,28},{28,32},{32,36}... | collective-permute-start | bytes 6291464 | tf_op jit(solution)/shard_map/ppermute | solution.py:14
  162.0 83.0 %collective-permute-start.7 = (f32[128,32,128]{2,0,1:T(8,128)S(1)}, f32[128,32,128]{2,0,1:T(8,128)S(1)}, u32[]{:S(2)}, u32[]{:S(2)}) collective-permute-start(f32[128,32,128]{2,0,1:T(8,128)S(1)} %get-tuple-element.243), channel_id=1, source_target_pairs={{0,8},{4,12},{8,16},{12,20},{16,24},{20,28},{24,32},{28,36},{32,40... | collective-permute-start | bytes 6291464 | tf_op jit(solution)/shard_map/ppermute | solution.py:14
  165.5 70.5 %collective-permute-start.2 = (f32[128,32]{0,1:T(8,128)S(1)}, f32[128,32]{0,1:T(8,128)S(1)}, u32[]{:S(2)}, u32[]{:S(2)}) collective-permute-start(f32[128,32]{0,1:T(8,128)S(1)} %get-tuple-element.246), channel_id=1, source_target_pairs={{0,4},{4,8},{8,12},{12,16},{16,20},{20,24},{24,28},{28,32},{32,36}... | collective-permute-start | bytes 49160 | tf_op jit(solution)/shard_map/ppermute | solution.py:14
  168.8 69.1 %collective-permute-start.3 = (f32[128,32]{0,1:T(8,128)S(1)}, f32[128,32]{0,1:T(8,128)S(1)}, u32[]{:S(2)}, u32[]{:S(2)}) collective-permute-start(f32[128,32]{0,1:T(8,128)S(1)} %get-tuple-element.245), channel_id=1, source_target_pairs={{0,4},{4,8},{8,12},{12,16},{16,20},{20,24},{24,28},{28,32},{32,36}... | collective-permute-start | bytes 49160 | tf_op jit(solution)/shard_map/ppermute | solution.py:14
  171.0 66.9 %collective-permute-start.5 = (f32[128,32]{0,1:T(8,128)S(1)}, f32[128,32]{0,1:T(8,128)S(1)}, u32[]{:S(2)}, u32[]{:S(2)}) collective-permute-start(f32[128,32]{0,1:T(8,128)S(1)} %get-tuple-element.247), channel_id=1, source_target_pairs={{0,8},{4,12},{8,16},{12,20},{16,24},{20,28},{24,32},{28,36},{32,40... | collective-permute-start | bytes 49160 | tf_op jit(solution)/shard_map/ppermute | solution.py:14
  236.0 8.9 %collective-permute-start.6 = (f32[128,32]{0,1:T(8,128)S(1)}, f32[128,32]{0,1:T(8,128)S(1)}, u32[]{:S(2)}, u32[]{:S(2)}) collective-permute-start(f32[128,32]{0,1:T(8,128)S(1)} %get-tuple-element.244), channel_id=1, source_target_pairs={{0,8},{4,12},{8,16},{12,20},{16,24},{20,28},{24,32},{28,36},{32,40... | collective-permute-start | bytes 49160 | tf_op jit(solution)/shard_map/ppermute | solution.py:14
Sparse Core Ops, SparseCore 0:
  9.5 88.8 all-gather.1
